TPU v7x, 32 devices: a whole 2x2x4 slice. The times are simulated.
32 devices in a mesh: groups: 2 (over x), wide: 16 (over z, y, core).
Axes of the slice: x: 2, y: 2, z: 4, core: 2. Of those that a mesh axis runs over, the one named last changes fastest.
Arguments:
- gen_cost: float32 [3072, 64], P(('groups', 'wide')), parts along dimension 0, may hold values from -6 to 6
- demand: float32 [20480, 64], P(('groups', 'wide')), parts along dimension 0, may hold values from -4 to 4
- ptdf_rows: bfloat16 [10240, 2048], P('wide'), may hold values from -0.15625 to 0.15625
- gen_zone: int32 [1536, 1], P('wide'), may hold values from 0 to 15; in each aligned block of 96 rows (0 to 95, 96 to 191, ...) at most 12 rows name the same one
- gen_local: int32 [1536], P('wide'), may hold values from 0 to 639
- gen_max: float32 [1536], P('wide'), may hold values from 0.3 to 3
- ramp_limit: float32 [1536], P('wide'), may hold values from 0.02 to 0.5
- line_limit: float32 [2048], replicated, may hold values from 0.1 to 1.5
- primal_start: float32 [3072, 64], P(('groups', 'wide')), parts along dimension 0, may hold values from 0 to 1
- balance_start: float32 [20480, 64], P(('groups', 'wide')), parts along dimension 0, may hold values from -4 to 4
- flow_start: float32 [128, 2048], P(('groups', 'wide')), parts along dimension 0, may hold values from -4 to 4
- ramp_start: float32 [3072, 64], P(('groups', 'wide')), parts along dimension 0, may hold values from -4 to 4
Outputs:
- primal: float32 [3072, 64], P(('groups', 'wide')), parts along dimension 0
- balance_dual: float32 [20480, 64], P(('groups', 'wide')), parts along dimension 0
- flow_dual: float32 [128, 2048], P(('groups', 'wide')), parts along dimension 0
- ramp_dual: float32 [3072, 64], P(('groups', 'wide')), parts along dimension 0
There are 2 independent parts, one for each index of `groups`. A program takes and returns all parts, laid end to end along the dimension named above; an argument that names none is the same for every part. Nothing has to cross between parts.
Inputs may be any that keep to these rules, and one draw needn't show every extreme that they name: `gen_zone`: among the 96 generators of one device (aligned blocks) at most 12 connect to one zone, and exactly 12 to some zone in some block.
All inputs are finite; a program needn't handle non-finite values.
Results may differ from a plain program's by a relative error of at most 0.0015.
Values may be sent and summed in bfloat16 or wider, within the bound.
A program may use at most 64 MiB of HBM per device.

v0:
```python
import jax
import jax.numpy as jnp
from jax import lax
from jax.sharding import PartitionSpec as P

ITERS = 3


step_primal = 0.25
step_dual = 0.25


def ramp_image(field):
    shifted = jnp.concatenate([field[:, :1], field[:, :-1]], axis=1)
    return field - shifted


def ramp_adjoint(dual):
    column = jnp.arange(dual.shape[1])[None, :]
    masked = jnp.where(column > 0, dual, jnp.float32(0.0))
    following = jnp.concatenate([masked[:, 1:], jnp.zeros_like(masked[:, :1])], axis=1)
    return masked - following


def contract_first(lhs_array, rhs_array):
    return lax.dot_general(
        lhs_array,
        rhs_array,
        (((0,), (0,)), ((), ())),
        preferred_element_type=jnp.float32,
        precision=lax.Precision.HIGHEST,
    )


def per_device(
    gen_cost,
    demand,
    ptdf_rows,
    gen_zone,
    gen_local,
    gen_max,
    ramp_limit,
    line_limit,
    primal_start,
    balance_start,
    flow_start,
    ramp_start,
):
    wide_count = lax.axis_size("wide")
    gen_dev, hour_count = primal_start.shape
    bus_dev = ptdf_rows.shape[0]
    hr_dev = flow_start.shape[0]
    capacity = max(2, 2 * gen_dev // wide_count)
    slot_count = wide_count * capacity
    zone_of = gen_zone[:, 0]
    member = (zone_of[:, None] == jnp.arange(wide_count)[None, :]).astype(jnp.int32)
    earlier = (jnp.arange(gen_dev)[:, None] > jnp.arange(gen_dev)[None, :]).astype(jnp.int32)
    ahead_counts = jnp.dot(earlier, member)
    rank_in_zone = jnp.sum(ahead_counts * member, axis=1)
    slot_of = zone_of * capacity + rank_in_zone
    packing_int = (jnp.arange(slot_count)[:, None] == slot_of[None, :]).astype(jnp.int32)
    packing = packing_int.astype(jnp.float32)
    send_ids = jnp.sum(packing_int * (gen_local + 1)[None, :], axis=1).reshape(wide_count, capacity)
    recv_ids = lax.all_to_all(send_ids, "wide", split_axis=0, concat_axis=0, tiled=True).reshape(
        slot_count
    )
    placing = (jnp.arange(bus_dev)[:, None] + 1 == recv_ids[None, :]).astype(jnp.float32)
    primal = primal_start
    balance = balance_start
    ramp_dual = ramp_start
    flow_state = lax.all_gather(flow_start, "wide", axis=0, tiled=True)
    for iteration in range(ITERS):
        flow_half = flow_state.astype(jnp.bfloat16)
        weighted = lax.dot_general(
            ptdf_rows, flow_half, (((1,), (1,)), ((), ())), preferred_element_type=jnp.float32
        )
        bus_dual = balance + weighted
        outgoing = contract_first(placing, bus_dual).reshape(wide_count, capacity, hour_count)
        returned = lax.all_to_all(
            outgoing, "wide", split_axis=0, concat_axis=0, tiled=True
        ).reshape(slot_count, hour_count)
        gen_dual = contract_first(packing, returned)
        moved = primal - step_primal * (gen_cost + gen_dual + ramp_adjoint(ramp_dual))
        primal_new = jnp.clip(moved, 0.0, gen_max[:, None])
        extra = 2.0 * primal_new - primal
        sending = jnp.dot(
            packing, extra, precision=lax.Precision.HIGHEST, preferred_element_type=jnp.float32
        )
        arrived = lax.all_to_all(
            sending.reshape(wide_count, capacity, hour_count),
            "wide",
            split_axis=0,
            concat_axis=0,
            tiled=True,
        )
        injection = jnp.dot(
            placing,
            arrived.reshape(slot_count, hour_count),
            precision=lax.Precision.HIGHEST,
            preferred_element_type=jnp.float32,
        )
        balance = balance + step_dual * (injection - demand)
        inj_half = injection.astype(jnp.bfloat16)
        term = lax.dot_general(
            inj_half, ptdf_rows, (((0,), (0,)), ((), ())), preferred_element_type=jnp.float32
        )
        flows = lax.psum(term, "wide")
        value = flow_state + step_dual * flows
        flow_state = value - step_dual * jnp.clip(
            value / step_dual, -line_limit[None, :], line_limit[None, :]
        )
        ramp_value = ramp_dual + step_dual * ramp_image(extra)
        ramp_dual = ramp_value - step_dual * jnp.clip(
            ramp_value / step_dual, -ramp_limit[:, None], ramp_limit[:, None]
        )
        primal = primal_new
    flow_out = lax.dynamic_slice_in_dim(flow_state, lax.axis_index("wide") * hr_dev, hr_dev, 0)
    return (primal, balance, flow_out, ramp_dual)


def solution(mesh):
    placed = (
        P(("groups", "wide"), None),
        P(("groups", "wide"), None),
        P("wide", None),
        P("wide", None),
        P("wide"),
        P("wide"),
        P("wide"),
        P(),
        P(("groups", "wide"), None),
        P(("groups", "wide"), None),
        P(("groups", "wide"), None),
        P(("groups", "wide"), None),
    )
    return jax.shard_map(
        per_device,
        mesh=mesh,
        in_specs=placed,
        out_specs=(
            P(("groups", "wide"), None),
            P(("groups", "wide"), None),
            P(("groups", "wide"), None),
            P(("groups", "wide"), None),
        ),
        check_vma=False,
    )
```

profile of v0, /device:TPU:0, one launch (start us, length us, event | category | flops | bytes accessed | tf_op | source)
XLA Modules:
  0.0 444.9 jit_solution(16869309983250194131)
XLA Ops:
  9.7 7.4 %all-to-all-start = ((s32[16,1,12]{2,1,0:T(1,128)}), s32[16,1,12]{2,1,0:T(1,128)S(1)}, u32[]{:S(2)}, u32[]{:S(2)}) async-start(s32[16,1,12]{2,1,0:T(1,128)} %bitcast.1), calls=%async_computation | async-start | bytes 16384 | tf_op jit(solution)/shard_map/all_to_all | solution.py:64
  17.1 24.9 %all-gather = f32[16,4,2048]{2,1,0:T(4,128)} all-gather(f32[1,4,2048]{2,1,0:T(4,128)} %bitcast.37), channel_id=1, replica_groups=mesh['groups'=2,'wide'=16] {'wide'}, dimensions={0}, use_global_device_ids=true | all-gather | bytes 557056 | tf_op jit(solution)/shard_map/all_gather | solution.py:71
  43.2 1.9 convolution_add_fusion
  47.7 3.5 all-to-all-start.1
  51.4 6.6 %all-to-all-done.1 = f32[16,1,768]{2,1,0:T(1,128)S(1)} async-done(((f32[16,1,768]{2,1,0:T(1,128)}), f32[16,1,768]{2,1,0:T(1,128)S(1)}, u32[]{:S(2)}, u32[]{:S(2)}) %all-to-all-start.1) | async-done | bytes 49184 | tf_op jit(solution)/shard_map/all_to_all | solution.py:79
  59.4 1.7 multiply_subtract_fusion.9
  63.7 10.2 %all_to_all.39 = f32[16,1,768]{2,1,0:T(1,128)S(1)} all-to-all(f32[16,1,768]{2,1,0:T(1,128)} %reshape.101), channel_id=1, replica_groups=mesh['groups'=2,'wide'=16] {'wide'}, dimensions={0} | all-to-all | bytes 98304 | tf_op jit(solution)/shard_map/all_to_all | solution.py:89
  82.0 85.1 %all-reduce.7.cloned.1.call-done = f32[64,2048]{1,0:T(8,128)} async-done(((f32[64,2048]{1,0:T(8,128)}), f32[64,2048]{1,0:T(8,128)}) %all-reduce.7.cloned.1.call-update) | async-done | bytes 524304 | tf_op jit(solution)/shard_map/psum | solution.py:107
  167.1 2.0 fusion.7
  173.6 5.2 %all-to-all-start.3 = ((f32[16,1,768]{2,1,0:T(1,128)}), f32[16,1,768]{2,1,0:T(1,128)}, u32[]{:S(2)}, u32[]{:S(2)}) async-start(f32[16,1,768]{2,1,0:T(1,128)} %reshape.103), calls=%async_computation.3 | async-start | bytes 98304 | tf_op jit(solution)/shard_map/all_to_all | solution.py:79
  181.5 4.2 all-to-all-done.3
  185.7 2.2 reduce.6
  190.9 1.9 multiply_subtract_fusion.7
  195.9 1.6 reshape.105
  197.5 10.9 %all_to_all.40 = f32[16,1,768]{2,1,0:T(1,128)} all-to-all(f32[16,1,768]{2,1,0:T(1,128)} %reshape.105), channel_id=1, replica_groups=mesh['groups'=2,'wide'=16] {'wide'}, dimensions={0} | all-to-all | bytes 98304 | tf_op jit(solution)/shard_map/all_to_all | solution.py:89
  208.4 2.2 reduce.7
  217.7 87.0 %all-reduce.9.cloned.1.call-done = f32[64,2048]{1,0:T(8,128)} async-done(((f32[64,2048]{1,0:T(8,128)}), f32[64,2048]{1,0:T(8,128)}) %all-reduce.9.cloned.1.call-update) | async-done | bytes 524304 | tf_op jit(solution)/shard_map/psum | solution.py:107
  306.9 2.0 fusion.6
  311.8 5.2 %all-to-all-start.5 = ((f32[16,1,768]{2,1,0:T(1,128)}), f32[16,1,768]{2,1,0:T(1,128)S(1)}, u32[]{:S(2)}, u32[]{:S(2)}) async-start(f32[16,1,768]{2,1,0:T(1,128)} %reshape.107), calls=%async_computation.5 | async-start | bytes 98304 | tf_op jit(solution)/shard_map/all_to_all | solution.py:79
  318.5 5.3 %all-to-all-done.5 = f32[16,1,768]{2,1,0:T(1,128)S(1)} async-done(((f32[16,1,768]{2,1,0:T(1,128)}), f32[16,1,768]{2,1,0:T(1,128)S(1)}, u32[]{:S(2)}, u32[]{:S(2)}) %all-to-all-start.5) | async-done | bytes 49184 | tf_op jit(solution)/shard_map/all_to_all | solution.py:79
  326.7 1.9 multiply_subtract_fusion.5
  331.7 10.2 %all_to_all.41 = f32[16,1,768]{2,1,0:T(1,128)S(1)} all-to-all(f32[16,1,768]{2,1,0:T(1,128)} %reshape.109), channel_id=1, replica_groups=mesh['groups'=2,'wide'=16] {'wide'}, dimensions={0} | all-to-all | bytes 98304 | tf_op jit(solution)/shard_map/all_to_all | solution.py:89
  344.8 2.1 multiply_add_fusion
  349.0 86.8 %all-reduce.11.cloned.1.call-done = f32[64,2048]{1,0:T(8,128)} async-done(((f32[64,2048]{1,0:T(8,128)}), f32[64,2048]{1,0:T(8,128)}) %all-reduce.11.cloned.1.call-update) | async-done | bytes 524304 | tf_op jit(solution)/shard_map/psum | solution.py:107
  (105 shorter events, 59.0 us)
Async XLA Ops:
  7.2 36.0 %copy-start = (bf16[640,2048]{1,0:T(8,128)(2,1)S(1)}, bf16[640,2048]{1,0:T(8,128)(2,1)}, u32[]{:S(2)}) copy-start(bf16[640,2048]{1,0:T(8,128)(2,1)} %param.14) | copy-start | bytes 7864324
  8.8 52.3 %copy-start.12 = (s32[96]{0:T(128)}, s32[96]{0:T(128)S(1)}, u32[]{:S(2)}) copy-start(s32[96]{0:T(128)S(1)} %get-tuple-element.16) | copy-start | bytes 1156
  9.7 35.4 %all-to-all-start = ((s32[16,1,12]{2,1,0:T(1,128)}), s32[16,1,12]{2,1,0:T(1,128)S(1)}, u32[]{:S(2)}, u32[]{:S(2)}) async-start(s32[16,1,12]{2,1,0:T(1,128)} %bitcast.1), calls=%async_computation | async-start | bytes 16384 | tf_op jit(solution)/shard_map/all_to_all | solution.py:64
  43.1 8.2 %copy-start.10 = (f32[96,64]{0,1:T(8,128)S(1)}, f32[96,64]{0,1:T(8,128)}, u32[]{:S(2)}) copy-start(f32[96,64]{0,1:T(8,128)} %param.23) | copy-start | bytes 73732
  43.2 16.2 %copy-start.6 = (f32[96,64]{0,1:T(8,128)S(1)}, f32[96,64]{0,1:T(8,128)}, u32[]{:S(2)}) copy-start(f32[96,64]{0,1:T(8,128)} %param.12) | copy-start | bytes 73732
  43.2 16.2 %copy-start.13 = (f32[96]{0:T(128)S(1)}, f32[96]{0:T(128)}, u32[]{:S(2)}) copy-start(f32[96]{0:T(128)} %param.17) | copy-start | bytes 1156
  45.1 31.1 %copy-start.16 = (pred[64]{0:T(512)(128)(4,1)}, pred[64]{0:T(512)(128)(4,1)S(1)}, u32[]{:S(2)}) copy-start(pred[64]{0:T(512)(128)(4,1)S(1)} %iota_compare_fusion.11) | copy-start | bytes 196
  47.7 10.2 %all-to-all-start.1 = ((f32[16,1,768]{2,1,0:T(1,128)}), f32[16,1,768]{2,1,0:T(1,128)S(1)}, u32[]{:S(2)}, u32[]{:S(2)}) async-start(f32[16,1,768]{2,1,0:T(1,128)} %reshape.99), calls=%async_computation.1 | async-start | bytes 98304 | tf_op jit(solution)/shard_map/all_to_all | solution.py:79
  51.3 115.8 %all-reduce.7.cloned.1.call-start = ((), (), s32[]{:S(2)}) async-start(), calls=%async_computation.7 | async-start | bytes 1048576 | tf_op jit(solution)/shard_map/psum | solution.py:107
  61.1 18.5 %copy-start.8 = (f32[2048]{0:T(1024)S(1)}, f32[2048]{0:T(1024)}, u32[]{:S(2)}) copy-start(f32[2048]{0:T(1024)} %param.19) | copy-start | bytes 24580
  61.1 106.0 %copy-start.1 = (f32[640,64]{0,1:T(8,128)S(1)}, f32[640,64]{0,1:T(8,128)}, u32[]{:S(2)}) copy-start(f32[640,64]{0,1:T(8,128)} %param.21) | copy-start | bytes 491524
  173.6 12.1 %all-to-all-start.3 = ((f32[16,1,768]{2,1,0:T(1,128)}), f32[16,1,768]{2,1,0:T(1,128)}, u32[]{:S(2)}, u32[]{:S(2)}) async-start(f32[16,1,768]{2,1,0:T(1,128)} %reshape.103), calls=%async_computation.3 | async-start | bytes 98304 | tf_op jit(solution)/shard_map/all_to_all | solution.py:79
  178.8 125.8 %all-reduce.9.cloned.1.call-start = ((), (), s32[]{:S(2)}) async-start(), calls=%async_computation.8 | async-start | bytes 1048576 | tf_op jit(solution)/shard_map/psum | solution.py:107
  180.3 0.6 copy-start.7
  215.1 0.7 copy-start.2
  306.1 0.8 copy-start.4
  306.9 37.9 %copy-start.3 = (f32[640,64]{0,1:T(8,128)S(1)}, f32[640,64]{0,1:T(8,128)}, u32[]{:S(2)}) copy-start(f32[640,64]{0,1:T(8,128)} %copy-done.2) | copy-start | bytes 491524
  306.9 37.9 %copy-start.5 = (f32[640,64]{0,1:T(8,128)S(1)}, f32[640,64]{0,1:T(8,128)}, u32[]{:S(2)}) copy-start(f32[640,64]{0,1:T(8,128)} %param.13) | copy-start | bytes 491524
  311.8 12.0 %all-to-all-start.5 = ((f32[16,1,768]{2,1,0:T(1,128)}), f32[16,1,768]{2,1,0:T(1,128)S(1)}, u32[]{:S(2)}, u32[]{:S(2)}) async-start(f32[16,1,768]{2,1,0:T(1,128)} %reshape.107), calls=%async_computation.5 | async-start | bytes 98304 | tf_op jit(solution)/shard_map/all_to_all | solution.py:79
  317.0 118.8 %all-reduce.11.cloned.1.call-start = ((), (), s32[]{:S(2)}) async-start(), calls=%async_computation.9 | async-start | bytes 1048576 | tf_op jit(solution)/shard_map/psum | solution.py:107
  341.9 6.4 %copy-start.11 = (f32[96,64]{0,1:T(8,128)S(1)}, f32[96,64]{0,1:T(8,128)}, u32[]{:S(2)}) copy-start(f32[96,64]{0,1:T(8,128)} %get-tuple-element.5) | copy-start | bytes 73732
  341.9 6.5 %copy-start.14 = (f32[96]{0:T(128)S(1)}, f32[96]{0:T(128)}, u32[]{:S(2)}) copy-start(f32[96]{0:T(128)} %param.18) | copy-start | bytes 1156
  341.9 6.5 %copy-start.15 = (f32[96]{0:T(128)S(1)}, f32[96]{0:T(128)}, u32[]{:S(2)}) copy-start(f32[96]{0:T(128)} %neg.13) | copy-start | bytes 1156
  346.9 89.9 %copy-start.9 = (f32[2048]{0:T(1024)S(1)}, f32[2048]{0:T(1024)}, u32[]{:S(2)}) copy-start(f32[2048]{0:T(1024)} %neg.12) | copy-start | bytes 24580
Sparse Core Ops, SparseCore 0:
  79.8 87.3 all-reduce.6
  217.3 87.3 all-reduce.8
  348.4 87.2 all-reduce.10
where the time goes:
time: 447 us; the launch traced here: 445 us
  waiting for transfers between devices  275 us (62%)
  blocking collectives  56.2 us (13%)
  local copies, waits for them, and re-layouts  29.6 us (7%)
  matrix products  28.6 us (6%)
  starting transfers between devices  21.5 us (5%)
  other arithmetic  20 us (4%)
  between operations  14.1 us (3%)
    psum x3, waiting for transfers between devices, per_device(): flows = lax.psum(term, 'wide')  259 us
    all_to_all x3, blocking collectives, per_device(): lax.all_to_all(sending.reshape(wide_count, capacity, hour_count), 'wide',...  31.3 us
    all_gather x1, blocking collectives, per_device(): flow_state = lax.all_gather(flow_start, 'wide', axis=0, tiled=True)  24.9 us
    all_to_all x3, waiting for transfers between devices, per_device(): lax.all_to_all(outgoing, 'wide', split_axis=0, concat_axis=0, tiled=True)  16 us
    unnamed x47, local copies, waits for them, and re-layouts  15.3 us
    all_to_all x3, starting transfers between devices, per_device(): lax.all_to_all(outgoing, 'wide', split_axis=0, concat_axis=0, tiled=True)  13.9 us
  transfers between devices with their start and end apart: 7, of which 6 were waited for; matrix products, arithmetic and copies ran while one was open for 2% of the time, Pallas kernels for 0%

commit v1 on v0

v1 whole, which is shorter than its diff:
```python
import functools

import jax
import jax.numpy as jnp
from jax import lax
from jax.experimental import pallas as pl
from jax.experimental.pallas import tpu as pltpu
from jax.sharding import PartitionSpec as P

ITERS = 3
STEP = 0.25
F32 = jnp.float32
BF16 = jnp.bfloat16
HIGH = lax.Precision.HIGHEST


def dot(a, b, dims=((1,), (0,)), precision=None):
    return lax.dot_general(a, b, (dims, ((), ())), preferred_element_type=F32, precision=precision)


def iota(shape, dim):
    return lax.broadcasted_iota(jnp.int32, shape, dim)


def shrink(value, limit):
    return value - STEP * jnp.clip(value * (1.0 / STEP), -limit, limit)


def kernel(
    n,
    cap,
    cost_ref,
    demand_ref,
    ptdf_hbm,
    zone_ref,
    local_ref,
    gmax_ref,
    rlim_ref,
    llim_ref,
    x_ref,
    yb_ref,
    yf_ref,
    yr_ref,
    x_out,
    yb_out,
    yf_out,
    yr_out,
    ptdf,
    payload,
    packed,
    arrived,
    turned,
    back,
    returned,
    part,
    cbuf,
    sbuf,
    rbuf,
    duals,
    fold_lim,
    fold_yf,
    in_sem,
    a_send,
    a_recv,
    b_send,
    b_recv,
    c_send,
    c_recv,
    r_send,
    r_recv,
    g_send,
    g_recv,
    f_send,
    f_recv,
):
    nc = n // 2
    gens, hours = cost_ref.shape
    buses, lines = ptdf.shape
    hr = yf_ref.shape[0]
    slots = n * cap
    folds = fold_yf.shape[0] // hr
    rows = hr * folds
    span = lines // folds
    me = lax.axis_index("wide")
    core = lax.rem(me, 2)
    chip = me // 2
    partner = chip * 2 + 1 - core

    def other(k):
        return lax.rem(me + k, n)

    def before(k):
        return lax.rem(me + n - k, n)

    def chip_after(k):
        return lax.rem(chip + k, nc)

    def chip_before(k):
        return lax.rem(chip + nc - k, nc)

    def remote(src, dst, send, recv, target):
        return pltpu.make_async_remote_copy(
            src_ref=src,
            dst_ref=dst,
            send_sem=send,
            recv_sem=recv,
            device_id={"wide": target},
            device_id_type=pl.DeviceIdType.MESH,
        )

    def loop(first, last, body):
        def step(k, carry):
            body(k)
            return carry

        lax.fori_loop(first, last, step, 0)

    barrier = pltpu.get_barrier_semaphore()

    def greet(k):
        pl.semaphore_signal(
            barrier, inc=1, device_id={"wide": other(k)}, device_id_type=pl.DeviceIdType.MESH
        )

    loop(1, n, greet)
    load = pltpu.make_async_copy(ptdf_hbm, ptdf, in_sem)
    load.start()

    for q in range(folds):
        cols = slice(q * span, (q + 1) * span)
        fold_yf[q * hr : (q + 1) * hr, :] = yf_ref[:, cols]
        fold_lim[q * hr : (q + 1) * hr, :] = jnp.broadcast_to(llim_ref[:, cols], (hr, span))

    def own_rows(c, ch):
        return pl.ds(pl.multiple_of((c * nc + ch) * rows, rows), rows)

    duals[0, own_rows(core, chip), :] = fold_yf[...].astype(BF16)

    zone = zone_ref[...]
    member = (zone == iota((gens, n), 1)).astype(F32)
    earlier = (iota((gens, gens), 0) > iota((gens, gens), 1)).astype(F32)
    ahead = dot(earlier.astype(BF16), member.astype(BF16))
    rank = jnp.sum(ahead * member, axis=1, keepdims=True).astype(jnp.int32)
    slot_col = zone * cap + rank
    eye = iota((gens, gens), 0) == iota((gens, gens), 1)
    slot_row = jnp.sum(
        jnp.where(eye, jnp.broadcast_to(slot_col.astype(F32), (gens, gens)), 0.0),
        axis=0,
        keepdims=True,
    ).astype(jnp.int32)

    def column(row):
        wide = jnp.broadcast_to(row, (gens, gens))
        return jnp.sum(jnp.where(eye, wide, 0.0), axis=1, keepdims=True)

    payload[...] = jnp.zeros_like(payload)
    payload[:, 0:hours] = cost_ref[...]
    payload[:, hours : 2 * hours] = x_ref[...]
    payload[:, 2 * hours : 3 * hours] = yr_ref[...]
    payload[:, 3 * hours : 3 * hours + 1] = column(gmax_ref[...])
    payload[:, 3 * hours + 1 : 3 * hours + 2] = column(rlim_ref[...])
    payload[:, 3 * hours + 2 : 3 * hours + 3] = column(local_ref[...].astype(F32)) + 1.0
    packing = (iota((slots, gens), 0) == slot_row).astype(F32)
    packed[...] = dot(packing, payload[...], precision=HIGH)

    pl.semaphore_wait(barrier, n - 1)

    def gather(it):
        mine = duals.at[it, own_rows(core, chip)]
        near = remote(mine, mine, f_send.at[it, 0], f_recv.at[it, 0], partner)
        near.start()

        def out(k):
            return remote(
                mine, mine, g_send.at[it, k], g_recv.at[it, k], chip_after(k) * 2 + core
            )

        loop(1, nc, lambda k: out(k).start())

    def gather_end(it):
        def into(k, c):
            return duals.at[it, own_rows(c, chip_before(k))]

        def forward(k):
            got = into(k, core)
            remote(got, got, g_send.at[it, k], g_recv.at[it, k], partner).wait_recv()
            remote(got, got, f_send.at[it, k], f_recv.at[it, k], partner).start()

        loop(1, nc, forward)

        def finish(k):
            got = into(k, 1 - core)
            remote(got, got, f_send.at[it, k], f_recv.at[it, k], partner).wait_recv()

        loop(0, nc, finish)

    def gather_sent(it):
        mine = duals.at[it, own_rows(core, chip)]
        remote(mine, mine, f_send.at[it, 0], f_recv.at[it, 0], partner).wait_send()

        def sent(k):
            remote(mine, mine, g_send.at[it, k], g_recv.at[it, k], partner).wait_send()
            got = duals.at[it, own_rows(core, chip_before(k))]
            remote(got, got, f_send.at[it, k], f_recv.at[it, k], partner).wait_send()

        loop(1, nc, sent)

    def rows_of(w):
        return pl.ds(pl.multiple_of(w * cap, cap), cap)

    def exchange(src, dst, send, recv):
        def go(k):
            remote(
                src.at[rows_of(other(k))], dst.at[rows_of(me)], send.at[k], recv.at[k], other(k)
            ).start()

        loop(1, n, go)
        dst[rows_of(me), :] = src[rows_of(me), :]

    def exchange_end(src, dst, send, recv):
        def end(k):
            remote(
                src.at[rows_of(other(k))],
                dst.at[rows_of(before(k))],
                send.at[k],
                recv.at[k],
                other(k),
            ).wait()

        loop(1, n, end)

    exchange(packed, arrived, a_send, a_recv)
    gather(0)
    exchange_end(packed, arrived, a_send, a_recv)

    ids = arrived[:, 3 * hours + 2 : 3 * hours + 3].astype(jnp.int32)
    turned[...] = arrived[...].T
    cost = turned[0:hours, :]
    x = turned[hours : 2 * hours, :]
    yr = turned[2 * hours : 3 * hours, :]
    gmax = turned[3 * hours : 3 * hours + 1, :]
    rlim = turned[3 * hours + 1 : 3 * hours + 2, :]
    id_row = turned[3 * hours + 2 : 3 * hours + 3, :].astype(jnp.int32)
    at_bus = (iota((slots, buses), 1) + 1 == ids).astype(F32)
    same_bool = (ids == id_row) & (ids > 0)
    same = same_bool.astype(F32)
    repeats = jnp.max(
        jnp.where(iota((slots, slots), 0) < iota((slots, slots), 1), same, 0.0),
        axis=0,
        keepdims=True,
    )
    lead = jnp.where((repeats == 0.0) & (id_row > 0), 1.0, 0.0)
    yb_slot = dot(at_bus, yb_ref[...], precision=HIGH).T
    demand_slot = dot(at_bus, demand_ref[...], precision=HIGH).T
    load.wait()
    at_bus16 = at_bus.astype(BF16)
    rows16 = [
        dot(at_bus16, ptdf[:, q * span : (q + 1) * span]).astype(BF16) for q in range(folds)
    ]

    piece_row = iota((n * rows, hours), 0)
    block = piece_row // rows
    owner = lax.rem(block, nc) * 2 + block // nc
    within = lax.rem(piece_row, rows)
    hour_of = owner * hr + lax.rem(within, hr)
    fold_of = within // hr
    at_hour = hour_of == iota((n * rows, hours), 1)
    spread = [(at_hour & (fold_of == q)).astype(F32).astype(BF16) for q in range(folds)]
    t_row = iota((hours, n * rows), 1)
    t_block = t_row // rows
    t_owner = lax.rem(t_block, nc) * 2 + t_block // nc
    t_within = lax.rem(t_row, rows)
    t_at = (t_owner * hr + lax.rem(t_within, hr)) == iota((hours, n * rows), 0)
    collect = [(t_at & (t_within // hr == q)).astype(F32).astype(BF16) for q in range(folds)]

    hour = iota((hours, slots), 0)
    total = jnp.zeros((hours, slots), F32)
    for it in range(ITERS):
        gather_end(it)
        gen_dual = yb_slot
        for q in range(folds):
            line16 = dot(collect[q], duals[it]).astype(BF16)
            gen_dual = gen_dual + dot(line16, rows16[q], ((1,), (1,)))
        masked = jnp.where(hour > 0, yr, 0.0)
        following = jnp.where(hour < hours - 1, pltpu.roll(masked, hours - 1, 0), 0.0)
        moved = x - STEP * (cost + gen_dual + (masked - following))
        x_new = jnp.clip(moved, 0.0, gmax)
        extra = 2.0 * x_new - x
        injection = dot(extra, same, precision=HIGH)
        inj16 = (injection * lead).astype(BF16)
        mixed = None
        for q in range(folds):
            term = dot(dot(spread[q], inj16).astype(BF16), rows16[q])
            mixed = term if mixed is None else mixed + term
        part[it] = mixed

        def give(k):
            return remote(
                part.at[it, own_rows(1 - core, chip_after(k))],
                cbuf.at[it, k],
                c_send.at[it, k],
                c_recv.at[it, k],
                partner,
            )

        def spoke(k):
            return remote(
                sbuf.at[it, k],
                rbuf.at[it, k],
                r_send.at[it, k],
                r_recv.at[it, k],
                chip_after(k) * 2 + core,
            )

        loop(1, nc, lambda k: give(k).start())
        give(0).start()

        total = total + injection
        yb_slot = yb_slot + STEP * (injection - demand_slot)
        change = jnp.where(hour > 0, extra - pltpu.roll(extra, 1, 0), 0.0)
        yr = shrink(yr + STEP * change, rlim)
        x = x_new

        def pass_on(k):
            give(k).wait_recv()
            sbuf[it, k] = part[it, own_rows(core, chip_after(k)), :] + cbuf[it, k]
            spoke(k).start()

        loop(1, nc, pass_on)
        give(0).wait_recv()
        mine = part[it, own_rows(core, chip), :] + cbuf[it, 0]
        if it == ITERS - 1:
            back[...] = jnp.concatenate([x, yr], axis=0).T
            exchange(back, returned, b_send, b_recv)
            placing = (iota((buses, slots), 0) + 1 == id_row).astype(F32) * lead
            placed = dot(placing, total.T, precision=HIGH)
            yb_out[...] = yb_ref[...] + STEP * (placed - ITERS * demand_ref[...])

        def add(k, acc):
            spoke(k).wait_recv()
            return acc + rbuf[it, k]

        flows = lax.fori_loop(1, nc, add, mine)
        fold_yf[...] = shrink(fold_yf[...] + STEP * flows, fold_lim[...])
        if it < ITERS - 1:
            duals[it + 1, own_rows(core, chip), :] = fold_yf[...].astype(BF16)
            gather(it + 1)

    for q in range(folds):
        yf_out[:, q * span : (q + 1) * span] = fold_yf[q * hr : (q + 1) * hr, :]
    exchange_end(back, returned, b_send, b_recv)
    unpack = (iota((gens, slots), 1) == slot_col).astype(F32)
    result = dot(unpack, returned[...], precision=HIGH)
    x_out[...] = result[:, 0:hours]
    yr_out[...] = result[:, hours : 2 * hours]

    for it in range(ITERS):
        gather_sent(it)

        def done(k):
            remote(
                part.at[it, own_rows(1 - core, chip_after(k))],
                cbuf.at[it, k],
                c_send.at[it, k],
                c_recv.at[it, k],
                partner,
            ).wait_send()

        loop(0, nc, done)

        def done_far(k):
            remote(
                sbuf.at[it, k], rbuf.at[it, k], r_send.at[it, k], r_recv.at[it, k], partner
            ).wait_send()

        loop(1, nc, done_far)


def per_device(
    gen_cost,
    demand,
    ptdf_rows,
    gen_zone,
    gen_local,
    gen_max,
    ramp_limit,
    line_limit,
    primal_start,
    balance_start,
    flow_start,
    ramp_start,
):
    n = lax.axis_size("wide")
    nc = n // 2
    gens, hours = primal_start.shape
    buses, lines = ptdf_rows.shape
    hr = flow_start.shape[0]
    cap = -(-max(2, 2 * gens // n) // 8) * 8
    slots = n * cap
    folds = max(1, 16 // hr)
    rows = hr * folds
    span = lines // folds
    width = -(-(3 * hours + 3) // 128) * 128
    vmem = pl.BlockSpec(memory_space=pltpu.VMEM)
    dma = pltpu.SemaphoreType.DMA
    shape = jax.ShapeDtypeStruct
    return pl.pallas_call(
        functools.partial(kernel, n, cap),
        out_shape=(
            shape(primal_start.shape, F32),
            shape(balance_start.shape, F32),
            shape(flow_start.shape, F32),
            shape(ramp_start.shape, F32),
        ),
        in_specs=[vmem, vmem, pl.BlockSpec(memory_space=pl.ANY)] + [vmem] * 9,
        out_specs=(vmem,) * 4,
        scratch_shapes=[
            pltpu.VMEM((buses, lines), BF16),
            pltpu.VMEM((gens, width), F32),
            pltpu.VMEM((slots, width), F32),
            pltpu.VMEM((slots, width), F32),
            pltpu.VMEM((width, slots), F32),
            pltpu.VMEM((slots, 2 * hours), F32),
            pltpu.VMEM((slots, 2 * hours), F32),
            pltpu.VMEM((ITERS, n * rows, span), F32),
            pltpu.VMEM((ITERS, nc, rows, span), F32),
            pltpu.VMEM((ITERS, nc, rows, span), F32),
            pltpu.VMEM((ITERS, nc, rows, span), F32),
            pltpu.VMEM((ITERS, n * rows, span), BF16),
            pltpu.VMEM((rows, span), F32),
            pltpu.VMEM((rows, span), F32),
            dma(()),
            dma((n,)),
            dma((n,)),
            dma((n,)),
            dma((n,)),
        ]
        + [dma((ITERS, nc))] * 8,
        compiler_params=pltpu.CompilerParams(
            collective_id=0, has_side_effects=True, vmem_limit_bytes=56 * 1024 * 1024
        ),
    )(
        gen_cost,
        demand,
        ptdf_rows,
        gen_zone,
        gen_local.reshape(1, gens),
        gen_max.reshape(1, gens),
        ramp_limit.reshape(1, gens),
        line_limit.reshape(1, lines),
        primal_start,
        balance_start,
        flow_start,
        ramp_start,
    )


def solution(mesh):
    both = P(("groups", "wide"), None)
    placed = (
        both,
        both,
        P("wide", None),
        P("wide", None),
        P("wide"),
        P("wide"),
        P("wide"),
        P(),
        both,
        both,
        both,
        both,
    )
    return jax.shard_map(
        per_device, mesh=mesh, in_specs=placed, out_specs=(both,) * 4, check_vma=False
    )
```

time: 447 us -> 85.1 us (0.19)
  waiting for transfers between devices: 275 us -> 0 us
  Pallas kernels: 0 us -> 68.3 us
  blocking collectives: 56.2 us -> 0 us
  matrix products: 28.6 us -> 0 us
  starting transfers between devices: 21.5 us -> 0 us
  other arithmetic: 20 us -> 0 us
  local copies, waits for them, and re-layouts: 29.6 us -> 15.6 us
  between operations: 14.1 us -> 0.64 us
    psum x3 -> x0, waiting for transfers between devices: 259 us -> none  [per_device(): flows = lax.psum(term, 'wide')]
    pallas_call x0 -> x1, Pallas kernels: none -> 68.3 us  [per_device(): pl.pallas_call(functools.partial(kernel, n, cap), out_shape=(shape(primal...]
    all_to_all x3 -> x0, blocking collectives: 31.3 us -> none  [per_device(): lax.all_to_all(sending.reshape(wide_count, capacity, hour_count), 'wide',...]
    dot_general x19 -> x0, matrix products: 28.6 us -> none  [the longest x6 8.64 us: contract_first(): lax.dot_general(lhs_array, rhs_array, (((0,), (0,)), ((), ())), preferred...]
    all_gather x1 -> x0, blocking collectives: 24.9 us -> none  [per_device(): flow_state = lax.all_gather(flow_start, 'wide', axis=0, tiled=True)]
    all_to_all x4 -> x0, starting transfers between devices: 21.3 us -> none  [the longest x3 13.9 us: per_device(): lax.all_to_all(outgoing, 'wide', split_axis=0, concat_axis=0, tiled=True)]
    all_to_all x4 -> x0, waiting for transfers between devices: 16 us -> none  [the longest x3 16 us: per_device(): lax.all_to_all(outgoing, 'wide', split_axis=0, concat_axis=0, tiled=True)]
    reshape x12 -> x0, local copies, waits for them, and re-layouts: 10.9 us -> none  [the longest x3 3.36 us: per_device(): sending.reshape(wide_count, capacity, hour_count)]
  transfers between devices with their start and end apart: 7 -> 0, of which waited for: 6 -> 0; matrix products, arithmetic and copies ran while one was open for 2% -> 0% of each run, Pallas kernels for 0% -> 0%
where the time goes in v1:
time: 85.1 us; the launch traced here: 84.5 us
  Pallas kernels  68.3 us (80%)
  local copies, waits for them, and re-layouts  15.6 us (18%)
    pallas_call x1, Pallas kernels, per_device(): pl.pallas_call(functools.partial(kernel, n, cap), out_shape=(shape(primal...  68.3 us
    unnamed x7, local copies, waits for them, and re-layouts  10.8 us
    pallas_call x3, local copies, waits for them, and re-layouts, per_device(): pl.pallas_call(functools.partial(kernel, n, cap), out_shape=(shape(primal...  4.78 us

profile of v1, /device:TPU:0, one launch (start us, length us, event | category | flops | bytes accessed | tf_op | source)
XLA Modules:
  0.0 84.5 jit_solution(3132578161131870842)
XLA Ops:
  0.6 1.5 %copy.16.cost_ref = f32[96,64]{1,0:T(8,128)} copy(f32[96,64]{0,1:T(8,128)} %param.12) | data formatting | bytes 49152 | tf_op args[0]
  2.1 1.4 %copy.18.zone_ref = s32[96,1]{1,0:T(8,128)} copy(s32[96,1]{0,1:T(1,128)} %param.15) | data formatting | bytes 768 | tf_op args[3]
  3.5 1.5 %copy.19.x_ref = f32[96,64]{1,0:T(8,128)} copy(f32[96,64]{0,1:T(8,128)} %param.20) | data formatting | bytes 49152 | tf_op args[8]
  4.9 1.5 %copy.21.yr_ref = f32[96,64]{1,0:T(8,128)} copy(f32[96,64]{0,1:T(8,128)} %param.23) | data formatting | bytes 49152 | tf_op args[11]
  6.4 1.8 %copy.17.demand_ref = f32[640,64]{1,0:T(8,128)} copy(f32[640,64]{0,1:T(8,128)} %param.13) | data formatting | bytes 327680 | tf_op args[1]
  8.2 1.8 %copy.20.yb_ref = f32[640,64]{1,0:T(8,128)} copy(f32[640,64]{0,1:T(8,128)} %param.21) | data formatting | bytes 327680 | tf_op args[9]
  10.0 68.3 %shard_map.147 = (f32[96,64]{1,0:T(8,128)}, f32[640,64]{1,0:T(8,128)}, f32[4,2048]{1,0:T(4,128)}, f32[96,64]{1,0:T(8,128)}) custom-call(f32[96,64]{1,0:T(8,128)} %copy.16.cost_ref, f32[640,64]{1,0:T(8,128)} %copy.17.demand_ref, bf16[640,2048]{1,0:T(8,128)(2,1)} %ptdf_hbm.1, s32[96,1]{1,0:T(8,128)} %copy.18.zone_ref, s32[1,96]{1,0:T(1,128)} %bitcast.5, ...), custom_call_target="tpu_custom_call" | custom-call | tf_op jit(solution)/shard_map/pallas_call | solution.py:407
  78.4 1.5 %copy.22 = f32[96,64]{0,1:T(8,128)} copy(f32[96,64]{1,0:T(8,128)} %get-tuple-element.4) | data formatting | bytes 49152 | tf_op jit(solution)/shard_map/pallas_call | solution.py:407
  79.9 1.5 %copy.24 = f32[96,64]{0,1:T(8,128)} copy(f32[96,64]{1,0:T(8,128)} %get-tuple-element.7) | data formatting | bytes 49152 | tf_op jit(solution)/shard_map/pallas_call | solution.py:407
  81.4 1.8 %copy.23 = f32[640,64]{0,1:T(8,128)} copy(f32[640,64]{1,0:T(8,128)} %get-tuple-element.5) | data formatting | bytes 327680 | tf_op jit(solution)/shard_map/pallas_call | solution.py:407
  83.2 1.4 %copy.26 = f32[4,2048]{1,0:T(4,128)} copy(f32[4,2048]{1,0:T(4,128)} %get-tuple-element.14) | data formatting | bytes 65536

commit v2 on v1

--- a/solution.py
+++ b/solution.py
@@ -74,7 +74,7 @@
     f_recv,
 ):
     nc = n // 2
-    gens, hours = cost_ref.shape
+    hours, gens = cost_ref.shape
     buses, lines = ptdf.shape
     hr = yf_ref.shape[0]
     slots = n * cap
@@ -137,31 +137,24 @@
     duals[0, own_rows(core, chip), :] = fold_yf[...].astype(BF16)
 
     zone = zone_ref[...]
-    member = (zone == iota((gens, n), 1)).astype(F32)
-    earlier = (iota((gens, gens), 0) > iota((gens, gens), 1)).astype(F32)
-    ahead = dot(earlier.astype(BF16), member.astype(BF16))
-    rank = jnp.sum(ahead * member, axis=1, keepdims=True).astype(jnp.int32)
-    slot_col = zone * cap + rank
-    eye = iota((gens, gens), 0) == iota((gens, gens), 1)
-    slot_row = jnp.sum(
-        jnp.where(eye, jnp.broadcast_to(slot_col.astype(F32), (gens, gens)), 0.0),
-        axis=0,
-        keepdims=True,
-    ).astype(jnp.int32)
-
-    def column(row):
-        wide = jnp.broadcast_to(row, (gens, gens))
-        return jnp.sum(jnp.where(eye, wide, 0.0), axis=1, keepdims=True)
+    member = (iota((n, gens), 0) == zone).astype(F32)
+    earlier = (iota((gens, gens), 0) < iota((gens, gens), 1)).astype(F32)
+    ahead = dot(member.astype(BF16), earlier.astype(BF16))
+    rank = jnp.sum(ahead * member, axis=0, keepdims=True).astype(jnp.int32)
+    lanes = payload.shape[1]
+    slot_of = jnp.concatenate(
+        [zone * cap + rank, jnp.full((1, lanes - gens), -1, jnp.int32)], axis=1
+    )
+    packing = (iota((slots, lanes), 0) == slot_of).astype(F32)
 
     payload[...] = jnp.zeros_like(payload)
-    payload[:, 0:hours] = cost_ref[...]
-    payload[:, hours : 2 * hours] = x_ref[...]
-    payload[:, 2 * hours : 3 * hours] = yr_ref[...]
-    payload[:, 3 * hours : 3 * hours + 1] = column(gmax_ref[...])
-    payload[:, 3 * hours + 1 : 3 * hours + 2] = column(rlim_ref[...])
-    payload[:, 3 * hours + 2 : 3 * hours + 3] = column(local_ref[...].astype(F32)) + 1.0
-    packing = (iota((slots, gens), 0) == slot_row).astype(F32)
-    packed[...] = dot(packing, payload[...], precision=HIGH)
+    payload[0:hours, 0:gens] = cost_ref[...]
+    payload[hours : 2 * hours, 0:gens] = x_ref[...]
+    payload[2 * hours : 3 * hours, 0:gens] = yr_ref[...]
+    payload[3 * hours : 3 * hours + 1, 0:gens] = gmax_ref[...]
+    payload[3 * hours + 1 : 3 * hours + 2, 0:gens] = rlim_ref[...]
+    payload[3 * hours + 2 : 3 * hours + 3, 0:gens] = local_ref[...].astype(F32) + 1.0
+    packed[...] = dot(packing, payload[...], ((1,), (1,)), HIGH)
 
     pl.semaphore_wait(barrier, n - 1)
 
@@ -250,8 +243,8 @@
         keepdims=True,
     )
     lead = jnp.where((repeats == 0.0) & (id_row > 0), 1.0, 0.0)
-    yb_slot = dot(at_bus, yb_ref[...], precision=HIGH).T
-    demand_slot = dot(at_bus, demand_ref[...], precision=HIGH).T
+    yb_slot = dot(at_bus, yb_ref[...].T, precision=HIGH).T
+    demand_slot = dot(at_bus, demand_ref[...].T, precision=HIGH).T
     load.wait()
     at_bus16 = at_bus.astype(BF16)
     rows16 = [
@@ -332,8 +325,7 @@
         if it == ITERS - 1:
             back[...] = jnp.concatenate([x, yr], axis=0).T
             exchange(back, returned, b_send, b_recv)
-            placing = (iota((buses, slots), 0) + 1 == id_row).astype(F32) * lead
-            placed = dot(placing, total.T, precision=HIGH)
+            placed = dot(total * lead, at_bus, precision=HIGH)
             yb_out[...] = yb_ref[...] + STEP * (placed - ITERS * demand_ref[...])
 
         def add(k, acc):
@@ -349,10 +341,9 @@
     for q in range(folds):
         yf_out[:, q * span : (q + 1) * span] = fold_yf[q * hr : (q + 1) * hr, :]
     exchange_end(back, returned, b_send, b_recv)
-    unpack = (iota((gens, slots), 1) == slot_col).astype(F32)
-    result = dot(unpack, returned[...], precision=HIGH)
-    x_out[...] = result[:, 0:hours]
-    yr_out[...] = result[:, hours : 2 * hours]
+    result = dot(returned[...].T, packing, precision=HIGH)
+    x_out[...] = result[0:hours, 0:gens]
+    yr_out[...] = result[hours : 2 * hours, 0:gens]
 
     for it in range(ITERS):
         gather_sent(it)
@@ -374,6 +365,15 @@
             ).wait_send()
 
         loop(1, nc, done_far)
+
+
+def hand_on(*refs):
+    sems = refs[8]
+    copies = [pltpu.make_async_copy(refs[i], refs[4 + i], sems.at[i]) for i in range(4)]
+    for copy in copies:
+        copy.start()
+    for copy in copies:
+        copy.wait()
 
 
 def per_device(
@@ -404,19 +404,19 @@
     vmem = pl.BlockSpec(memory_space=pltpu.VMEM)
     dma = pltpu.SemaphoreType.DMA
     shape = jax.ShapeDtypeStruct
-    return pl.pallas_call(
+    results = pl.pallas_call(
         functools.partial(kernel, n, cap),
         out_shape=(
-            shape(primal_start.shape, F32),
-            shape(balance_start.shape, F32),
+            shape((hours, gens), F32),
+            shape((hours, buses), F32),
             shape(flow_start.shape, F32),
-            shape(ramp_start.shape, F32),
+            shape((hours, gens), F32),
         ),
         in_specs=[vmem, vmem, pl.BlockSpec(memory_space=pl.ANY)] + [vmem] * 9,
         out_specs=(vmem,) * 4,
         scratch_shapes=[
             pltpu.VMEM((buses, lines), BF16),
-            pltpu.VMEM((gens, width), F32),
+            pltpu.VMEM((width, -(-gens // 128) * 128), F32),
             pltpu.VMEM((slots, width), F32),
             pltpu.VMEM((slots, width), F32),
             pltpu.VMEM((width, slots), F32),
@@ -440,19 +440,28 @@
             collective_id=0, has_side_effects=True, vmem_limit_bytes=56 * 1024 * 1024
         ),
     )(
-        gen_cost,
-        demand,
+        gen_cost.T,
+        demand.T,
         ptdf_rows,
-        gen_zone,
+        gen_zone.reshape(1, gens),
         gen_local.reshape(1, gens),
         gen_max.reshape(1, gens),
         ramp_limit.reshape(1, gens),
         line_limit.reshape(1, lines),
-        primal_start,
-        balance_start,
+        primal_start.T,
+        balance_start.T,
         flow_start,
-        ramp_start,
+        ramp_start.T,
     )
+    anywhere = pl.BlockSpec(memory_space=pltpu.HBM)
+    primal, balance, flow, ramp = pl.pallas_call(
+        hand_on,
+        out_shape=tuple(shape(r.shape, F32) for r in results),
+        in_specs=[anywhere] * 4,
+        out_specs=(anywhere,) * 4,
+        scratch_shapes=[dma((4,))],
+    )(*results)
+    return primal.T, balance.T, flow, ramp.T
 
 
 def solution(mesh):

time: 85.1 us -> 77.9 us (0.915)
  local copies, waits for them, and re-layouts: 15.6 us -> 0 us
  Pallas kernels: 68.3 us -> 77.1 us
    unnamed x7 -> x0, local copies, waits for them, and re-layouts: 10.8 us -> none
    pallas_call x1 -> x2, Pallas kernels: 68.3 us -> 77.1 us  [the longest x1 68 us: per_device(): pl.pallas_call(functools.partial(kernel, n, cap), out_shape=(shape((hours...]
    pallas_call x3 -> x0, local copies, waits for them, and re-layouts: 4.78 us -> none  [per_device(): pl.pallas_call(functools.partial(kernel, n, cap), out_shape=(shape(primal...]
where the time goes in v2:
time: 77.9 us; the launch traced here: 77.8 us
  Pallas kernels  77.1 us (99%)
    pallas_call x1, Pallas kernels, per_device(): pl.pallas_call(functools.partial(kernel, n, cap), out_shape=(shape((hours...  68 us
    pallas_call x1, Pallas kernels, per_device(): pl.pallas_call(hand_on, out_shape=tuple((shape(r.shape, F32) for r in res...  9.08 us

profile of v2, /device:TPU:0, one launch (start us, length us, event | category | flops | bytes accessed | tf_op | source)
XLA Modules:
  0.0 77.8 jit_solution(9877943503257270666)
XLA Ops:
  0.6 68.0 %shard_map.147 = (f32[64,96]{1,0:T(8,128)}, f32[64,640]{1,0:T(8,128)}, f32[4,2048]{1,0:T(4,128)}, f32[64,96]{1,0:T(8,128)}) custom-call(f32[64,96]{1,0:T(8,128)} %bitcast.15, f32[64,640]{1,0:T(8,128)} %bitcast.13, bf16[640,2048]{1,0:T(8,128)(2,1)} %ptdf_hbm.1, s32[1,96]{1,0:T(1,128)} %bitcast.19, s32[1,96]{1,0:T(1,128)} %bitcast.20, f32[1,96]{1,0:T(1,128)} %bitcast.21, ...), custom_call_target="tpu_custom_call" | custom-call | tf_op jit(solution)/shard_map/pallas_call | solution.py:407
  68.7 9.1 %shard_map.148 = (f32[64,96]{1,0:T(8,128)}, f32[64,640]{1,0:T(8,128)}, f32[4,2048]{1,0:T(4,128)}, f32[64,96]{1,0:T(8,128)}) custom-call(f32[64,96]{1,0:T(8,128)} %get-tuple-element.12.refs_0_, f32[64,640]{1,0:T(8,128)} %get-tuple-element.13.refs_1_, f32[4,2048]{1,0:T(4,128)} %get-tuple-element.14.refs_2_, f32[64,96]{1,0:T(8,128)} %get-tuple-element.15.refs_3_), custom_call_target="tpu_custom_call" | custom-call | tf_op jit(solution)/shard_map/pallas_call | solution.py:457

commit v3 on v2

--- a/solution.py
+++ b/solution.py
@@ -57,8 +57,10 @@
     sbuf,
     rbuf,
     duals,
-    fold_lim,
-    fold_yf,
+    near_rows,
+    state,
+    swap_out,
+    swap_in,
     in_sem,
     a_send,
     a_recv,
@@ -72,15 +74,18 @@
     g_recv,
     f_send,
     f_recv,
+    s_send,
+    s_recv,
 ):
     nc = n // 2
     hours, gens = cost_ref.shape
     buses, lines = ptdf.shape
     hr = yf_ref.shape[0]
     slots = n * cap
-    folds = fold_yf.shape[0] // hr
-    rows = hr * folds
-    span = lines // folds
+    tile = 2 * hr
+    rows = 2 * tile
+    half = lines // 2
+    span = half // 2
     me = lax.axis_index("wide")
     core = lax.rem(me, 2)
     chip = me // 2
@@ -126,15 +131,26 @@
     load = pltpu.make_async_copy(ptdf_hbm, ptdf, in_sem)
     load.start()
 
-    for q in range(folds):
-        cols = slice(q * span, (q + 1) * span)
-        fold_yf[q * hr : (q + 1) * hr, :] = yf_ref[:, cols]
-        fold_lim[q * hr : (q + 1) * hr, :] = jnp.broadcast_to(llim_ref[:, cols], (hr, span))
-
     def own_rows(c, ch):
         return pl.ds(pl.multiple_of((c * nc + ch) * rows, rows), rows)
 
-    duals[0, own_rows(core, chip), :] = fold_yf[...].astype(BF16)
+    def hours_of(ch):
+        return pl.ds(pl.multiple_of(ch * tile, tile), tile)
+
+    def pick(first, second):
+        return jnp.where(core == 0, first, second)
+
+    def swap(i):
+        return remote(swap_out.at[i], swap_in.at[i], s_send.at[i], s_recv.at[i], partner)
+
+    def keep_rounded(it):
+        now = state[...]
+        duals[it, own_rows(core, chip), :] = jnp.concatenate(
+            [now[:, :span], now[:, span:]], axis=0
+        ).astype(BF16)
+
+    limit = pick(llim_ref[:, :half], llim_ref[:, half:])
+    swap_out[0] = pick(yf_ref[:, half:], yf_ref[:, :half])
 
     zone = zone_ref[...]
     member = (iota((n, gens), 0) == zone).astype(F32)
@@ -170,19 +186,17 @@
 
         loop(1, nc, lambda k: out(k).start())
 
-    def gather_end(it):
-        def into(k, c):
-            return duals.at[it, own_rows(c, chip_before(k))]
-
+    def gather_far(it):
         def forward(k):
-            got = into(k, core)
+            got = duals.at[it, own_rows(core, chip_before(k))]
             remote(got, got, g_send.at[it, k], g_recv.at[it, k], partner).wait_recv()
             remote(got, got, f_send.at[it, k], f_recv.at[it, k], partner).start()
 
         loop(1, nc, forward)
 
+    def gather_near(it):
         def finish(k):
-            got = into(k, 1 - core)
+            got = duals.at[it, own_rows(1 - core, chip_before(k))]
             remote(got, got, f_send.at[it, k], f_recv.at[it, k], partner).wait_recv()
 
         loop(0, nc, finish)
@@ -222,7 +236,13 @@
 
         loop(1, n, end)
 
+    swap(0).start()
     exchange(packed, arrived, a_send, a_recv)
+    swap(0).wait()
+    held = pick(yf_ref[:, :half], yf_ref[:, half:])
+    state[0:hr, :] = pick(held, swap_in[0])
+    state[hr:tile, :] = pick(swap_in[0], held)
+    keep_rounded(0)
     gather(0)
     exchange_end(packed, arrived, a_send, a_recv)
 
@@ -243,37 +263,32 @@
         keepdims=True,
     )
     lead = jnp.where((repeats == 0.0) & (id_row > 0), 1.0, 0.0)
-    yb_slot = dot(at_bus, yb_ref[...].T, precision=HIGH).T
-    demand_slot = dot(at_bus, demand_ref[...].T, precision=HIGH).T
+    bus_rows = jnp.concatenate([yb_ref[...], demand_ref[...]], axis=0).T
+    slot_rows = dot(at_bus, bus_rows, precision=HIGH).T
+    yb_slot = slot_rows[0:hours, :]
+    demand_slot = slot_rows[hours : 2 * hours, :]
     load.wait()
     at_bus16 = at_bus.astype(BF16)
-    rows16 = [
-        dot(at_bus16, ptdf[:, q * span : (q + 1) * span]).astype(BF16) for q in range(folds)
-    ]
-
-    piece_row = iota((n * rows, hours), 0)
-    block = piece_row // rows
-    owner = lax.rem(block, nc) * 2 + block // nc
-    within = lax.rem(piece_row, rows)
-    hour_of = owner * hr + lax.rem(within, hr)
-    fold_of = within // hr
-    at_hour = hour_of == iota((n * rows, hours), 1)
-    spread = [(at_hour & (fold_of == q)).astype(F32).astype(BF16) for q in range(folds)]
-    t_row = iota((hours, n * rows), 1)
-    t_block = t_row // rows
-    t_owner = lax.rem(t_block, nc) * 2 + t_block // nc
-    t_within = lax.rem(t_row, rows)
-    t_at = (t_owner * hr + lax.rem(t_within, hr)) == iota((hours, n * rows), 0)
-    collect = [(t_at & (t_within // hr == q)).astype(F32).astype(BF16) for q in range(folds)]
+    for c in range(2):
+        near_rows[c] = dot(at_bus16, ptdf[:, c * half : (c + 1) * half]).astype(BF16)
+
+    def prices(it, c):
+        got = duals[it, pl.ds(pl.multiple_of(c * nc * rows, nc * rows), nc * rows), :]
+        got = got.astype(F32).reshape(nc, 2, tile, span)
+        sums = None
+        for u in range(2):
+            line16 = got[:, u].reshape(hours, span).astype(BF16)
+            term = dot(line16, near_rows[c, :, u * span : (u + 1) * span], ((1,), (1,)))
+            sums = term if sums is None else sums + term
+        return sums
 
     hour = iota((hours, slots), 0)
     total = jnp.zeros((hours, slots), F32)
     for it in range(ITERS):
-        gather_end(it)
-        gen_dual = yb_slot
-        for q in range(folds):
-            line16 = dot(collect[q], duals[it]).astype(BF16)
-            gen_dual = gen_dual + dot(line16, rows16[q], ((1,), (1,)))
+        gather_far(it)
+        gen_dual = yb_slot + prices(it, core)
+        gather_near(it)
+        gen_dual = gen_dual + prices(it, 1 - core)
         masked = jnp.where(hour > 0, yr, 0.0)
         following = jnp.where(hour < hours - 1, pltpu.roll(masked, hours - 1, 0), 0.0)
         moved = x - STEP * (cost + gen_dual + (masked - following))
@@ -281,15 +296,11 @@
         extra = 2.0 * x_new - x
         injection = dot(extra, same, precision=HIGH)
         inj16 = (injection * lead).astype(BF16)
-        mixed = None
-        for q in range(folds):
-            term = dot(dot(spread[q], inj16).astype(BF16), rows16[q])
-            mixed = term if mixed is None else mixed + term
-        part[it] = mixed
+        part[it, 1 - core] = dot(inj16, near_rows[1 - core])
 
         def give(k):
             return remote(
-                part.at[it, own_rows(1 - core, chip_after(k))],
+                part.at[it, 1 - core, hours_of(chip_after(k))],
                 cbuf.at[it, k],
                 c_send.at[it, k],
                 c_recv.at[it, k],
@@ -307,21 +318,22 @@
 
         loop(1, nc, lambda k: give(k).start())
         give(0).start()
+        part[it, core] = dot(inj16, near_rows[core])
+
+        def pass_on(k):
+            give(k).wait_recv()
+            sbuf[it, k] = part[it, core, hours_of(chip_after(k)), :] + cbuf[it, k]
+            spoke(k).start()
+
+        loop(1, nc, pass_on)
+        give(0).wait_recv()
+        mine = part[it, core, hours_of(chip), :] + cbuf[it, 0]
 
         total = total + injection
         yb_slot = yb_slot + STEP * (injection - demand_slot)
         change = jnp.where(hour > 0, extra - pltpu.roll(extra, 1, 0), 0.0)
         yr = shrink(yr + STEP * change, rlim)
         x = x_new
-
-        def pass_on(k):
-            give(k).wait_recv()
-            sbuf[it, k] = part[it, own_rows(core, chip_after(k)), :] + cbuf[it, k]
-            spoke(k).start()
-
-        loop(1, nc, pass_on)
-        give(0).wait_recv()
-        mine = part[it, own_rows(core, chip), :] + cbuf[it, 0]
         if it == ITERS - 1:
             back[...] = jnp.concatenate([x, yr], axis=0).T
             exchange(back, returned, b_send, b_recv)
@@ -333,24 +345,29 @@
             return acc + rbuf[it, k]
 
         flows = lax.fori_loop(1, nc, add, mine)
-        fold_yf[...] = shrink(fold_yf[...] + STEP * flows, fold_lim[...])
+        state[...] = shrink(state[...] + STEP * flows, limit)
         if it < ITERS - 1:
-            duals[it + 1, own_rows(core, chip), :] = fold_yf[...].astype(BF16)
+            keep_rounded(it + 1)
             gather(it + 1)
 
-    for q in range(folds):
-        yf_out[:, q * span : (q + 1) * span] = fold_yf[q * hr : (q + 1) * hr, :]
+    swap_out[1] = pick(state[hr:tile, :], state[0:hr, :])
+    swap(1).start()
     exchange_end(back, returned, b_send, b_recv)
     result = dot(returned[...].T, packing, precision=HIGH)
     x_out[...] = result[0:hours, 0:gens]
     yr_out[...] = result[hours : 2 * hours, 0:gens]
 
+    swap(1).wait()
+    held = pick(state[0:hr, :], state[hr:tile, :])
+    yf_out[:, :half] = pick(held, swap_in[1])
+    yf_out[:, half:] = pick(swap_in[1], held)
+
     for it in range(ITERS):
         gather_sent(it)
 
         def done(k):
             remote(
-                part.at[it, own_rows(1 - core, chip_after(k))],
+                part.at[it, 1 - core, hours_of(chip_after(k))],
                 cbuf.at[it, k],
                 c_send.at[it, k],
                 c_recv.at[it, k],
@@ -368,12 +385,8 @@
 
 
 def hand_on(*refs):
-    sems = refs[8]
-    copies = [pltpu.make_async_copy(refs[i], refs[4 + i], sems.at[i]) for i in range(4)]
-    for copy in copies:
-        copy.start()
-    for copy in copies:
-        copy.wait()
+    for i in range(4):
+        refs[4 + i][...] = refs[i][...]
 
 
 def per_device(
@@ -397,9 +410,8 @@
     hr = flow_start.shape[0]
     cap = -(-max(2, 2 * gens // n) // 8) * 8
     slots = n * cap
-    folds = max(1, 16 // hr)
-    rows = hr * folds
-    span = lines // folds
+    tile = 2 * hr
+    half = lines // 2
     width = -(-(3 * hours + 3) // 128) * 128
     vmem = pl.BlockSpec(memory_space=pltpu.VMEM)
     dma = pltpu.SemaphoreType.DMA
@@ -422,20 +434,23 @@
             pltpu.VMEM((width, slots), F32),
             pltpu.VMEM((slots, 2 * hours), F32),
             pltpu.VMEM((slots, 2 * hours), F32),
-            pltpu.VMEM((ITERS, n * rows, span), F32),
-            pltpu.VMEM((ITERS, nc, rows, span), F32),
-            pltpu.VMEM((ITERS, nc, rows, span), F32),
-            pltpu.VMEM((ITERS, nc, rows, span), F32),
-            pltpu.VMEM((ITERS, n * rows, span), BF16),
-            pltpu.VMEM((rows, span), F32),
-            pltpu.VMEM((rows, span), F32),
+            pltpu.VMEM((ITERS, 2, hours, half), F32),
+            pltpu.VMEM((ITERS, nc, tile, half), F32),
+            pltpu.VMEM((ITERS, nc, tile, half), F32),
+            pltpu.VMEM((ITERS, nc, tile, half), F32),
+            pltpu.VMEM((ITERS, n * 2 * tile, half // 2), BF16),
+            pltpu.VMEM((2, slots, half), BF16),
+            pltpu.VMEM((tile, half), F32),
+            pltpu.VMEM((2, hr, half), F32),
+            pltpu.VMEM((2, hr, half), F32),
             dma(()),
             dma((n,)),
             dma((n,)),
             dma((n,)),
             dma((n,)),
         ]
-        + [dma((ITERS, nc))] * 8,
+        + [dma((ITERS, nc))] * 8
+        + [dma((2,))] * 2,
         compiler_params=pltpu.CompilerParams(
             collective_id=0, has_side_effects=True, vmem_limit_bytes=56 * 1024 * 1024
         ),
@@ -453,13 +468,11 @@
         flow_start,
         ramp_start.T,
     )
-    anywhere = pl.BlockSpec(memory_space=pltpu.HBM)
     primal, balance, flow, ramp = pl.pallas_call(
         hand_on,
         out_shape=tuple(shape(r.shape, F32) for r in results),
-        in_specs=[anywhere] * 4,
-        out_specs=(anywhere,) * 4,
-        scratch_shapes=[dma((4,))],
+        in_specs=[vmem] * 4,
+        out_specs=(vmem,) * 4,
     )(*results)
     return primal.T, balance.T, flow, ramp.T
 

time: 77.9 us -> 67.5 us (0.87)
  Pallas kernels: 77.1 us -> 66.7 us
    pallas_call x1, Pallas kernels: 9.08 us -> 1.62 us  [per_device(): pl.pallas_call(hand_on, out_shape=tuple((shape(r.shape, F32) for r in res...]
    pallas_call x1, Pallas kernels: 68 us -> 65.1 us  [per_device(): pl.pallas_call(functools.partial(kernel, n, cap), out_shape=(shape((hours...]
where the time goes in v3:
time: 67.5 us; the launch traced here: 67.4 us
  Pallas kernels  66.7 us (99%)
    pallas_call x1, Pallas kernels, per_device(): pl.pallas_call(functools.partial(kernel, n, cap), out_shape=(shape((hours...  65.1 us
    pallas_call x1, Pallas kernels, per_device(): pl.pallas_call(hand_on, out_shape=tuple((shape(r.shape, F32) for r in res...  1.62 us

profile of v3, /device:TPU:0, one launch (start us, length us, event | category | flops | bytes accessed | tf_op | source)
XLA Modules:
  0.0 67.4 jit_solution(18099496777575282634)
XLA Ops:
  0.6 65.1 %shard_map.147 = (f32[64,96]{1,0:T(8,128)}, f32[64,640]{1,0:T(8,128)}, f32[4,2048]{1,0:T(4,128)}, f32[64,96]{1,0:T(8,128)}) custom-call(f32[64,96]{1,0:T(8,128)} %bitcast.15, f32[64,640]{1,0:T(8,128)} %bitcast.13, bf16[640,2048]{1,0:T(8,128)(2,1)} %ptdf_hbm.1, s32[1,96]{1,0:T(1,128)} %bitcast.19, s32[1,96]{1,0:T(1,128)} %bitcast.20, f32[1,96]{1,0:T(1,128)} %bitcast.21, ...), custom_call_target="tpu_custom_call" | custom-call | tf_op jit(solution)/shard_map/pallas_call | solution.py:419
  65.8 1.6 %shard_map.148 = (f32[64,96]{1,0:T(8,128)}, f32[64,640]{1,0:T(8,128)}, f32[4,2048]{1,0:T(4,128)}, f32[64,96]{1,0:T(8,128)}) custom-call(f32[64,96]{1,0:T(8,128)} %get-tuple-element.12.refs_0_, f32[64,640]{1,0:T(8,128)} %get-tuple-element.13.refs_1_, f32[4,2048]{1,0:T(4,128)} %get-tuple-element.14.refs_2_, f32[64,96]{1,0:T(8,128)} %get-tuple-element.15.refs_3_), custom_call_target="tpu_custom_call" | custom-call | tf_op jit(solution)/shard_map/pallas_call | solution.py:471

commit v4 on v3

--- a/solution.py
+++ b/solution.py
@@ -97,6 +97,14 @@
     def before(k):
         return lax.rem(me + n - k, n)
 
+    pairs = nc // 2
+    pair, side = chip // 2, lax.rem(chip, 2)
+
+    def chip_of(i):
+        to = i // pairs
+        where = to * side + (1 - to) * (1 - side)
+        return lax.rem(pair + lax.rem(i + 1, pairs), pairs) * 2 + where
+
     def chip_after(k):
         return lax.rem(chip + k, nc)
 
@@ -245,6 +253,7 @@
     keep_rounded(0)
     gather(0)
     exchange_end(packed, arrived, a_send, a_recv)
+    gather_far(0)
 
     ids = arrived[:, 3 * hours + 2 : 3 * hours + 3].astype(jnp.int32)
     turned[...] = arrived[...].T
@@ -285,7 +294,8 @@
     hour = iota((hours, slots), 0)
     total = jnp.zeros((hours, slots), F32)
     for it in range(ITERS):
-        gather_far(it)
+        if it > 0:
+            gather_far(it)
         gen_dual = yb_slot + prices(it, core)
         gather_near(it)
         gen_dual = gen_dual + prices(it, 1 - core)
@@ -300,34 +310,39 @@
 
         def give(k):
             return remote(
-                part.at[it, 1 - core, hours_of(chip_after(k))],
+                part.at[it, 1 - core, hours_of(chip_of(k))],
                 cbuf.at[it, k],
                 c_send.at[it, k],
                 c_recv.at[it, k],
                 partner,
             )
 
-        def spoke(k):
+        def spoke(k, target):
             return remote(
-                sbuf.at[it, k],
-                rbuf.at[it, k],
-                r_send.at[it, k],
-                r_recv.at[it, k],
-                chip_after(k) * 2 + core,
+                sbuf.at[it, k], rbuf.at[it, k], r_send.at[it, k], r_recv.at[it, k], target
             )
 
-        loop(1, nc, lambda k: give(k).start())
-        give(0).start()
+        loop(0, nc, lambda k: give(k).start())
         part[it, core] = dot(inj16, near_rows[core])
 
-        def pass_on(k):
+        def across(k):
             give(k).wait_recv()
-            sbuf[it, k] = part[it, core, hours_of(chip_after(k)), :] + cbuf[it, k]
-            spoke(k).start()
-
-        loop(1, nc, pass_on)
-        give(0).wait_recv()
-        mine = part[it, core, hours_of(chip), :] + cbuf[it, 0]
+            sbuf[it, k] = part[it, core, hours_of(chip_of(k)), :] + cbuf[it, k]
+            spoke(k, (pair * 2 + 1 - side) * 2 + core).start()
+
+        loop(0, pairs, across)
+
+        def along(k):
+            give(k).wait_recv()
+            spoke(k - pairs, partner).wait_recv()
+            own = part[it, core, hours_of(chip_of(k)), :] + cbuf[it, k]
+            sbuf[it, k] = own + rbuf[it, k - pairs]
+            spoke(k, chip_of(k) * 2 + core).start()
+
+        loop(pairs, nc - 1, along)
+        give(nc - 1).wait_recv()
+        spoke(pairs - 1, partner).wait_recv()
+        mine = part[it, core, hours_of(chip), :] + cbuf[it, nc - 1] + rbuf[it, pairs - 1]
 
         total = total + injection
         yb_slot = yb_slot + STEP * (injection - demand_slot)
@@ -341,10 +356,10 @@
             yb_out[...] = yb_ref[...] + STEP * (placed - ITERS * demand_ref[...])
 
         def add(k, acc):
-            spoke(k).wait_recv()
+            spoke(k, partner).wait_recv()
             return acc + rbuf[it, k]
 
-        flows = lax.fori_loop(1, nc, add, mine)
+        flows = lax.fori_loop(pairs, nc - 1, add, mine)
         state[...] = shrink(state[...] + STEP * flows, limit)
         if it < ITERS - 1:
             keep_rounded(it + 1)
@@ -367,7 +382,7 @@
 
         def done(k):
             remote(
-                part.at[it, 1 - core, hours_of(chip_after(k))],
+                part.at[it, 1 - core, hours_of(chip_of(k))],
                 cbuf.at[it, k],
                 c_send.at[it, k],
                 c_recv.at[it, k],
@@ -381,7 +396,7 @@
                 sbuf.at[it, k], rbuf.at[it, k], r_send.at[it, k], r_recv.at[it, k], partner
             ).wait_send()
 
-        loop(1, nc, done_far)
+        loop(0, nc - 1, done_far)
 
 
 def hand_on(*refs):

time: 67.5 us -> 69 us (1.022)
  Pallas kernels: 66.7 us -> 68.2 us
    pallas_call x1, Pallas kernels: 65.1 us -> 66.6 us  [per_device(): pl.pallas_call(functools.partial(kernel, n, cap), out_shape=(shape((hours...]
where the time goes in v4:
time: 69 us; the launch traced here: 68.8 us
  Pallas kernels  68.2 us (99%)
    pallas_call x1, Pallas kernels, per_device(): pl.pallas_call(functools.partial(kernel, n, cap), out_shape=(shape((hours...  66.6 us
    pallas_call x1, Pallas kernels, per_device(): pl.pallas_call(hand_on, out_shape=tuple((shape(r.shape, F32) for r in res...  1.62 us

profile of v4, /device:TPU:0, one launch (start us, length us, event | category | flops | bytes accessed | tf_op | source)
XLA Modules:
  0.0 68.8 jit_solution(3207070353025273325)
XLA Ops:
  0.6 66.6 %shard_map.147 = (f32[64,96]{1,0:T(8,128)}, f32[64,640]{1,0:T(8,128)}, f32[4,2048]{1,0:T(4,128)}, f32[64,96]{1,0:T(8,128)}) custom-call(f32[64,96]{1,0:T(8,128)} %bitcast.15, f32[64,640]{1,0:T(8,128)} %bitcast.13, bf16[640,2048]{1,0:T(8,128)(2,1)} %ptdf_hbm.1, s32[1,96]{1,0:T(1,128)} %bitcast.19, s32[1,96]{1,0:T(1,128)} %bitcast.20, f32[1,96]{1,0:T(1,128)} %bitcast.21, ...), custom_call_target="tpu_custom_call" | custom-call | tf_op jit(solution)/shard_map/pallas_call | solution.py:434
  67.2 1.6 %shard_map.148 = (f32[64,96]{1,0:T(8,128)}, f32[64,640]{1,0:T(8,128)}, f32[4,2048]{1,0:T(4,128)}, f32[64,96]{1,0:T(8,128)}) custom-call(f32[64,96]{1,0:T(8,128)} %get-tuple-element.12.refs_0_, f32[64,640]{1,0:T(8,128)} %get-tuple-element.13.refs_1_, f32[4,2048]{1,0:T(4,128)} %get-tuple-element.14.refs_2_, f32[64,96]{1,0:T(8,128)} %get-tuple-element.15.refs_3_), custom_call_target="tpu_custom_call" | custom-call | tf_op jit(solution)/shard_map/pallas_call | solution.py:486

commit v5 on v3

--- a/solution.py
+++ b/solution.py
@@ -49,6 +49,8 @@
     payload,
     packed,
     arrived,
+    packed_ids,
+    arrived_ids,
     turned,
     back,
     returned,
@@ -76,6 +78,8 @@
     f_recv,
     s_send,
     s_recv,
+    i_send,
+    i_recv,
 ):
     nc = n // 2
     hours, gens = cost_ref.shape
@@ -170,7 +174,10 @@
     payload[3 * hours : 3 * hours + 1, 0:gens] = gmax_ref[...]
     payload[3 * hours + 1 : 3 * hours + 2, 0:gens] = rlim_ref[...]
     payload[3 * hours + 2 : 3 * hours + 3, 0:gens] = local_ref[...].astype(F32) + 1.0
-    packed[...] = dot(packing, payload[...], ((1,), (1,)), HIGH)
+    split = packed.shape[1]
+    filled = dot(packing, payload[...], ((1,), (1,)), HIGH)
+    packed[...] = filled[:, :split]
+    packed_ids[...] = filled[:, split:]
 
     pl.semaphore_wait(barrier, n - 1)
 
@@ -237,22 +244,19 @@
         loop(1, n, end)
 
     swap(0).start()
-    exchange(packed, arrived, a_send, a_recv)
+    exchange(packed_ids, arrived_ids, i_send, i_recv)
     swap(0).wait()
     held = pick(yf_ref[:, :half], yf_ref[:, half:])
     state[0:hr, :] = pick(held, swap_in[0])
     state[hr:tile, :] = pick(swap_in[0], held)
     keep_rounded(0)
     gather(0)
-    exchange_end(packed, arrived, a_send, a_recv)
-
-    ids = arrived[:, 3 * hours + 2 : 3 * hours + 3].astype(jnp.int32)
-    turned[...] = arrived[...].T
-    cost = turned[0:hours, :]
-    x = turned[hours : 2 * hours, :]
-    yr = turned[2 * hours : 3 * hours, :]
-    gmax = turned[3 * hours : 3 * hours + 1, :]
-    rlim = turned[3 * hours + 1 : 3 * hours + 2, :]
+    exchange(packed, arrived, a_send, a_recv)
+    exchange_end(packed_ids, arrived_ids, i_send, i_recv)
+
+    id_column = 3 * hours + 2 - split
+    ids = arrived_ids[:, id_column : id_column + 1].astype(jnp.int32)
+    turned[split:, :] = arrived_ids[...].T
     id_row = turned[3 * hours + 2 : 3 * hours + 3, :].astype(jnp.int32)
     at_bus = (iota((slots, buses), 1) + 1 == ids).astype(F32)
     same_bool = (ids == id_row) & (ids > 0)
@@ -289,6 +293,14 @@
         gen_dual = yb_slot + prices(it, core)
         gather_near(it)
         gen_dual = gen_dual + prices(it, 1 - core)
+        if it == 0:
+            exchange_end(packed, arrived, a_send, a_recv)
+            turned[0:split, :] = arrived[...].T
+            cost = turned[0:hours, :]
+            x = turned[hours : 2 * hours, :]
+            yr = turned[2 * hours : 3 * hours, :]
+            gmax = turned[3 * hours : 3 * hours + 1, :]
+            rlim = turned[3 * hours + 1 : 3 * hours + 2, :]
         masked = jnp.where(hour > 0, yr, 0.0)
         following = jnp.where(hour < hours - 1, pltpu.roll(masked, hours - 1, 0), 0.0)
         moved = x - STEP * (cost + gen_dual + (masked - following))
@@ -429,8 +441,10 @@
         scratch_shapes=[
             pltpu.VMEM((buses, lines), BF16),
             pltpu.VMEM((width, -(-gens // 128) * 128), F32),
-            pltpu.VMEM((slots, width), F32),
-            pltpu.VMEM((slots, width), F32),
+            pltpu.VMEM((slots, width - 128), F32),
+            pltpu.VMEM((slots, width - 128), F32),
+            pltpu.VMEM((slots, 128), F32),
+            pltpu.VMEM((slots, 128), F32),
             pltpu.VMEM((width, slots), F32),
             pltpu.VMEM((slots, 2 * hours), F32),
             pltpu.VMEM((slots, 2 * hours), F32),
@@ -450,7 +464,8 @@
             dma((n,)),
         ]
         + [dma((ITERS, nc))] * 8
-        + [dma((2,))] * 2,
+        + [dma((2,))] * 2
+        + [dma((n,))] * 2,
         compiler_params=pltpu.CompilerParams(
             collective_id=0, has_side_effects=True, vmem_limit_bytes=56 * 1024 * 1024
         ),

time: 67.5 us -> 66.9 us (level)
  no operation moved by 1% of the time
where the time goes in v5:
time: 66.9 us; the launch traced here: 66.8 us
  Pallas kernels  66.1 us (99%)
    pallas_call x1, Pallas kernels, per_device(): pl.pallas_call(functools.partial(kernel, n, cap), out_shape=(shape((hours...  64.5 us
    pallas_call x1, Pallas kernels, per_device(): pl.pallas_call(hand_on, out_shape=tuple((shape(r.shape, F32) for r in res...  1.62 us

profile of v5, /device:TPU:0, one launch (start us, length us, event | category | flops | bytes accessed | tf_op | source)
XLA Modules:
  0.0 66.8 jit_solution(14886193104712866352)
XLA Ops:
  0.6 64.5 %shard_map.147 = (f32[64,96]{1,0:T(8,128)}, f32[64,640]{1,0:T(8,128)}, f32[4,2048]{1,0:T(4,128)}, f32[64,96]{1,0:T(8,128)}) custom-call(f32[64,96]{1,0:T(8,128)} %bitcast.15, f32[64,640]{1,0:T(8,128)} %bitcast.13, bf16[640,2048]{1,0:T(8,128)(2,1)} %ptdf_hbm.1, s32[1,96]{1,0:T(1,128)} %bitcast.19, s32[1,96]{1,0:T(1,128)} %bitcast.20, f32[1,96]{1,0:T(1,128)} %bitcast.21, ...), custom_call_target="tpu_custom_call" | custom-call | tf_op jit(solution)/shard_map/pallas_call | solution.py:431
  65.2 1.6 %shard_map.148 = (f32[64,96]{1,0:T(8,128)}, f32[64,640]{1,0:T(8,128)}, f32[4,2048]{1,0:T(4,128)}, f32[64,96]{1,0:T(8,128)}) custom-call(f32[64,96]{1,0:T(8,128)} %get-tuple-element.12.refs_0_, f32[64,640]{1,0:T(8,128)} %get-tuple-element.13.refs_1_, f32[4,2048]{1,0:T(4,128)} %get-tuple-element.14.refs_2_, f32[64,96]{1,0:T(8,128)} %get-tuple-element.15.refs_3_), custom_call_target="tpu_custom_call" | custom-call | tf_op jit(solution)/shard_map/pallas_call | solution.py:486
